TPU v7x, 32 devices: a whole 2x2x4 slice. The times are simulated.
32 devices in a mesh: occ: 8 (over z, x), aux: 4 (over y, core).
Axes of the slice: x: 2, y: 2, z: 4, core: 2. Of those that a mesh axis runs over, the one named last changes fastest.
Arguments:
- factors: bfloat16 [16, 256, 1024], P('occ', None, 'aux'), may hold values from -0.8984375 to 0.8984375
- occ_energy: float32 [16], replicated, may hold values from -3 to -0.5
- vir_energy: float32 [256], replicated, may hold values from 0.5 to 3
- i_slot: int32 [256], P('occ'), may hold values from 0 to 1
- j_slot: int32 [256], P('occ'), may hold values from 0 to 1
- partner_device: int32 [256, 1], P('occ'), may hold values from 0 to 7; in each aligned block of 32 rows (0 to 31, 32 to 63, ...) at most 6 rows name the same one
- pair_count: int32 [8], P('occ'), may hold values from 1 to 32, 230 in all
Outputs:
- gamma: float32 [16, 256, 1024], P('occ', None, 'aux')
- aux_matrix: float32 [1024, 1024], P('aux', 'occ')
Inputs may be any that keep to these rules, and one draw needn't show every extreme that they name: `partner_device`: among the 32 pair slots of one occ index, at most 6 name the same partner device, and some index reaches 6.
All inputs are finite; a program needn't handle non-finite values. No bound on the sum of `pair_count` on one device may be relied on, other than what follows from the above.
Results may differ from a plain program's by a relative error of at most 0.0013.
Values may be sent and summed in bfloat16 or wider, within the bound.
A program may use at most 128 MiB of HBM per device.

v0:
```python
import jax
import jax.numpy as jnp
from jax import lax
from jax.sharding import PartitionSpec as P


def body(factors, occ_energy, vir_energy, i_slot, j_slot, partner_device, pair_count):
    held, virtuals, columns = factors.shape
    pair_slots = i_slot.shape[0]
    occ_count = lax.axis_size("occ")
    capacity = max(2, (3 * pair_slots // 2 + occ_count - 1) // occ_count)
    slot_total = occ_count * capacity
    device_index = lax.axis_index("occ")
    pair_order = jnp.arange(pair_slots, dtype=jnp.int32)
    living = pair_order < pair_count[0]
    target = partner_device[:, 0]
    earlier = (
        (target[:, None] == target[None, :])
        & living[None, :]
        & (pair_order[None, :] < pair_order[:, None])
    )
    slot_rank = jnp.sum(earlier.astype(jnp.int32), axis=1)
    slot_index = target * capacity + slot_rank
    slot_hit = (slot_index[:, None] == jnp.arange(slot_total, dtype=jnp.int32)[None, :]) & living[
        :, None
    ]
    requests = jnp.sum(jnp.where(slot_hit, j_slot[:, None] + 1, 0), axis=0) - 1
    wanted = lax.all_to_all(requests, "occ", split_axis=0, concat_axis=0, tiled=True)
    wanted_hit = (wanted[:, None] == jnp.arange(held, dtype=jnp.int32)[None, :]).astype(
        jnp.bfloat16
    )
    far_index = target * held + j_slot
    piece = lax.all_gather(factors, "occ", axis=0, tiled=True)
    count = piece.shape[0]
    hit = (far_index[:, None] == jnp.arange(count, dtype=jnp.int32)[None, :]).astype(jnp.bfloat16)
    gathered = jnp.dot(
        hit, piece.reshape(count, virtuals * columns), preferred_element_type=jnp.float32
    )
    partner_blocks = gathered.astype(jnp.bfloat16).reshape(pair_slots, virtuals, columns)
    own_blocks = factors[i_slot]
    orbitals = occ_energy.shape[0]
    table = jnp.arange(orbitals, dtype=jnp.int32)
    own_index = device_index * held + i_slot
    energy_own = jnp.sum(
        jnp.where(own_index[:, None] == table[None, :], occ_energy[None, :], 0.0), axis=1
    )
    energy_far = jnp.sum(
        jnp.where(far_index[:, None] == table[None, :], occ_energy[None, :], 0.0), axis=1
    )
    denominator = (
        vir_energy[None, :, None]
        + vir_energy[None, None, :]
        - energy_own[:, None, None]
        - energy_far[:, None, None]
    )
    partial_value = jnp.einsum(
        "pvq,pwq->pvw", own_blocks, partner_blocks, preferred_element_type=jnp.float32
    )
    summed = lax.psum(partial_value, "aux")
    amplitude = jnp.where(living[:, None, None], summed / denominator, 0.0).astype(jnp.bfloat16)
    local_terms = jnp.einsum(
        "pvw,pwq->pvq", amplitude, partner_blocks, preferred_element_type=jnp.float32
    )
    owner_hit = (i_slot[:, None] == jnp.arange(held, dtype=jnp.int32)[None, :]).astype(jnp.float32)
    gamma_local = jnp.einsum("po,pvq->ovq", owner_hit, local_terms, precision=lax.Precision.HIGHEST)
    return_terms = jnp.einsum(
        "pwv,pwq->pvq", amplitude, own_blocks, preferred_element_type=jnp.float32
    ).astype(jnp.bfloat16)
    placed = jnp.dot(
        slot_hit.astype(jnp.bfloat16).T,
        return_terms.reshape(pair_slots, virtuals * columns),
        preferred_element_type=jnp.float32,
    )
    placed = placed.astype(jnp.bfloat16).reshape(slot_total, virtuals, columns)
    returned = lax.all_to_all(placed, "occ", split_axis=0, concat_axis=0, tiled=True)
    gathered_back = jnp.dot(
        wanted_hit.T,
        returned.reshape(slot_total, virtuals * columns),
        preferred_element_type=jnp.float32,
    )
    gamma = gamma_local + gathered_back.reshape(held, virtuals, columns)
    rounded = gamma.astype(jnp.bfloat16)
    stacked = jnp.stack([rounded, factors])
    gamma_rows = rounded.reshape(held * virtuals, columns)
    factor_flat = factors.reshape(held * virtuals, columns)
    piece = lax.all_gather(stacked, "aux", axis=3, tiled=True)
    width_here = piece.shape[3]
    gamma_piece = piece[0].reshape(held * virtuals, width_here)
    factor_piece = piece[1].reshape(held * virtuals, width_here)
    first = jnp.dot(gamma_rows.T, factor_piece, preferred_element_type=jnp.float32)
    second = jnp.dot(factor_flat.T, gamma_piece, preferred_element_type=jnp.float32)
    terms = first + second
    shared = lax.psum_scatter(terms, "occ", scatter_dimension=1, tiled=True)
    factor_scale = float(orbitals * virtuals) ** (-0.5)
    return (gamma, shared * factor_scale)


def solution(mesh):
    placed = (P("occ", None, "aux"), P(), P(), P("occ"), P("occ"), P("occ", None), P("occ"))
    return jax.shard_map(
        body,
        mesh=mesh,
        in_specs=placed,
        out_specs=(P("occ", None, "aux"), P("aux", "occ")),
        check_vma=False,
    )
```

profile of v0, /device:TPU:3, one launch (start us, length us, event | category | flops | bytes accessed | tf_op | source)
XLA Modules:
  0.0 495.3 jit_solution(15083597723668897939)
XLA Ops:
  8.6 3.7 gather_fusion
  12.4 46.3 %all-gather.3.cloned.1.call-done = bf16[16,256,256]{2,1,0:T(8,128)(2,1)} async-done(((bf16[2,256,256]{2,1,0:T(8,128)(2,1)}), bf16[16,256,256]{2,1,0:T(8,128)(2,1)}) %all-gather.3.cloned.1.call-update) | async-done | bytes 2097168 | tf_op jit(solution)/shard_map/all_gather | solution.py:33
  58.7 2.8 copy.44
  61.4 1.3 convolution_convert_fusion.1
  63.7 2.0 copy-done.3
  65.7 4.5 fusion.26
  71.9 5.0 %all-to-all-start = ((s32[8,6,1]{1,2,0:T(1,128)}), s32[8,6,1]{1,2,0:T(1,128)S(1)}, u32[]{:S(2)}, u32[]{:S(2)}) async-start(s32[8,6,1]{1,2,0:T(1,128)} %bitcast.5), calls=%async_computation | async-start | bytes 8192 | tf_op jit(solution)/shard_map/all_to_all | solution.py:28
  77.2 146.5 %all-reduce.2.cloned.1.call-done = f32[32,256,256]{2,1,0:T(8,128)} async-done(((f32[32,256,256]{2,1,0:T(8,128)}), f32[32,256,256]{2,1,0:T(8,128)}) %all-reduce.2.cloned.1.call-update) | async-done | bytes 8388624 | tf_op jit(solution)/shard_map/psum | solution.py:59
  223.7 4.5 select_convert_fusion
  228.3 1.3 convolution_convert_fusion.2
  230.3 2.5 copy.46
  232.7 1.9 convolution_convert_fusion
  234.6 4.1 copy.47
  238.7 5.6 %all-to-all-start.1 = ((bf16[48,256,256]{2,1,0:T(8,128)(2,1)}), bf16[48,256,256]{2,1,0:T(8,128)(2,1)}, u32[]{:S(2)}, u32[]{:S(2)}) async-start(bf16[48,256,256]{2,1,0:T(8,128)(2,1)} %bitcast.66), calls=%async_computation.1 | async-start | bytes 12582912 | tf_op jit(solution)/shard_map/all_to_all | solution.py:75
  245.9 7.9 %fusion.27 = f32[32,256,256]{2,1,0:T(8,128)} fusion(bf16[32,256,256]{2,1,0:T(8,128)(2,1)} %copy-done.2, bf16[32,256,256]{2,1,0:T(8,128)(2,1)} %bitcast.65), kind=kOutput, calls=%fused_computation.51 | convolution fusion | flops 1073741824 | bytes 16777216 | tf_op jit(solution)/shard_map/pvw,pwq->pvq/dot_general | solution.py:61
  253.9 127.9 %all-to-all-done.1 = bf16[48,256,256]{2,1,0:T(8,128)(2,1)} async-done(((bf16[48,256,256]{2,1,0:T(8,128)(2,1)}), bf16[48,256,256]{2,1,0:T(8,128)(2,1)}, u32[]{:S(2)}, u32[]{:S(2)}) %all-to-all-start.1) | async-done | bytes 6291488 | tf_op jit(solution)/shard_map/all_to_all | solution.py:75
  381.8 6.4 %fusion.2 = f32[2,256,256]{2,0,1:T(2,128)S(1)} fusion(s32[48]{0:T(128)S(1)} %eq.105, bf16[6,8,256,256]{3,2,1,0:T(8,128)(2,1)} %bitcast.25), kind=kOutput, calls=%fused_computation.6 | convolution fusion | flops 12583008 | bytes 6815936 | tf_op jit(solution)/shard_map/dot_general | solution.py:76
  388.3 8.0 %fusion.25 = (bf16[2,256,256]{2,0,1:T(2,128)(2,1)S(1)}, f32[2,256,256]{2,0,1:T(2,128)S(1)}) fusion(f32[2,256,256]{2,0,1:T(2,128)S(1)} %fusion.2, f32[32,256,256]{2,1,0:T(8,128)S(1)} %copy-done.1, s32[32]{0:T(128)S(1)} %copy-done.8), kind=kOutput, calls=%fused_computation.48 | convolution fusion | flops 50593856 | bytes 9699456 | tf_op jit(solution)/shard_map/po,pvq->ovq/dot_general | solution.py:65
  396.2 1.6 pad_maximum_fusion
  397.9 22.7 %all-gather.5.cloned.1.call-done = bf16[2,2,256,1024]{3,1,2,0:T(2,128)(2,1)} async-done(((bf16[2,2,256,256]{3,1,2,0:T(2,128)(2,1)}), bf16[2,2,256,1024]{3,1,2,0:T(2,128)(2,1)}) %all-gather.5.cloned.1.call-update) | async-done | bytes 2097168 | tf_op jit(solution)/shard_map/all_gather | solution.py:86
  420.6 2.7 fusion.24
  424.3 1.5 fusion.5
  426.6 60.6 %reduce-scatter.2.cloned.1.call-done = f32[256,128]{1,0:T(8,128)} async-done(((f32[256,1024]{1,0:T(8,128)}), f32[256,128]{1,0:T(8,128)}) %reduce-scatter.2.cloned.1.call-update) | async-done | bytes 131088 | tf_op jit(solution)/shard_map/reduce_scatter | solution.py:93
  487.2 1.6 broadcast_multiply_fusion
  (51 shorter events, 7.9 us)
Async XLA Ops:
  7.2 51.5 %all-gather.3.cloned.1.call-start = ((), (), s32[]{:S(2)}) async-start(), calls=%async_computation.3 | async-start | bytes 2359296 | tf_op jit(solution)/shard_map/all_gather | solution.py:33
  7.9 215.8 %all-reduce.2.cloned.1.call-start = ((), (), s32[]{:S(2)}) async-start(), calls=%async_computation.4 | async-start | bytes 16777216 | tf_op jit(solution)/shard_map/psum | solution.py:59
  8.6 3.7 copy-start.6
  8.6 3.7 copy-start.10
  62.7 3.0 copy-start.4
  63.7 2.0 copy-start.3
  70.2 6.7 %copy-start.9 = (f32[16]{0:T(128)S(1)}, f32[16]{0:T(128)}, u32[]{:S(2)}) copy-start(f32[16]{0:T(128)} %param.8) | copy-start | bytes 196
  70.3 6.8 %copy-start.7 = (f32[256]{0:T(256)S(1)}, f32[256]{0:T(256)}, u32[]{:S(2)}) copy-start(f32[256]{0:T(256)} %param.9) | copy-start | bytes 3076
  71.9 166.8 %all-to-all-start = ((s32[8,6,1]{1,2,0:T(1,128)}), s32[8,6,1]{1,2,0:T(1,128)S(1)}, u32[]{:S(2)}, u32[]{:S(2)}) async-start(s32[8,6,1]{1,2,0:T(1,128)} %bitcast.5), calls=%async_computation | async-start | bytes 8192 | tf_op jit(solution)/shard_map/all_to_all | solution.py:28
  223.7 4.6 copy-start.5
  228.3 2.0 copy-start.2
  238.7 5.6 %copy-start = (bf16[2,256,256]{2,1,0:T(8,128)(2,1)S(1)}, bf16[2,256,256]{2,1,0:T(8,128)(2,1)}, u32[]{:S(2)}) copy-start(bf16[2,256,256]{2,1,0:T(8,128)(2,1)} %param.7) | copy-start | bytes 786436
  238.7 143.1 %all-to-all-start.1 = ((bf16[48,256,256]{2,1,0:T(8,128)(2,1)}), bf16[48,256,256]{2,1,0:T(8,128)(2,1)}, u32[]{:S(2)}, u32[]{:S(2)}) async-start(bf16[48,256,256]{2,1,0:T(8,128)(2,1)} %bitcast.66), calls=%async_computation.1 | async-start | bytes 12582912 | tf_op jit(solution)/shard_map/all_to_all | solution.py:75
  244.4 176.2 %all-gather.5.cloned.1.call-start = ((), (), s32[]{:S(2)}) async-start(), calls=%async_computation.5 | async-start | bytes 2621440 | tf_op jit(solution)/shard_map/all_gather | solution.py:86
  381.8 6.4 %copy-start.1 = (f32[32,256,256]{2,1,0:T(8,128)S(1)}, f32[32,256,256]{2,1,0:T(8,128)}, u32[]{:S(2)}) copy-start(f32[32,256,256]{2,1,0:T(8,128)} %fusion.27) | copy-start | bytes 25165828
  381.8 6.4 %copy-start.8 = (s32[32]{0:T(128)S(1)}, s32[32]{0:T(128)}, u32[]{:S(2)}) copy-start(s32[32]{0:T(128)} %param.10) | copy-start | bytes 388
  397.8 89.4 %reduce-scatter.2.cloned.1.call-start = ((), (), s32[]{:S(2)}) async-start(), calls=%async_computation.6 | async-start | bytes 1179648 | tf_op jit(solution)/shard_map/reduce_scatter | solution.py:93
Sparse Core Ops, SparseCore 0:
  10.1 48.4 all-gather.2
  70.4 153.2 all-reduce.1
  397.9 22.6 all-gather.4
  425.9 61.2 reduce-scatter.1
where the time goes:
time: 499 us; the launch traced here: 495 us
  waiting for transfers between devices  405 us (81%)
  matrix products  33.3 us (7%)
  local copies, waits for them, and re-layouts  22.4 us (4%)
  between operations  14.6 us (3%)
  starting transfers between devices  10.8 us (2%)
  other arithmetic  9.44 us (2%)
    psum x1, waiting for transfers between devices, body(): summed = lax.psum(partial_value, 'aux')  147 us
    all_to_all x1, waiting for transfers between devices, body(): lax.all_to_all(placed, 'occ', split_axis=0, concat_axis=0, tiled=True)  128 us
    reduce_scatter x1, waiting for transfers between devices, body(): shared = lax.psum_scatter(terms, 'occ', scatter_dimension=1, tiled=True)  60.6 us
    all_gather x1, waiting for transfers between devices, body(): piece = lax.all_gather(factors, 'occ', axis=0, tiled=True)  46.3 us
    all_gather x1, waiting for transfers between devices, body(): piece = lax.all_gather(stacked, 'aux', axis=3, tiled=True)  22.7 us
    unnamed x28, local copies, waits for them, and re-layouts  14.2 us
  transfers between devices with their start and end apart: 6, of which 5 were waited for; matrix products, arithmetic and copies ran while one was open for 6% of the time, Pallas kernels for 0%

commit v1 on v0

--- a/solution.py
+++ b/solution.py
@@ -1,10 +1,16 @@
 import jax
 import jax.numpy as jnp
 from jax import lax
+from jax.experimental import pallas as pl
+from jax.experimental.pallas import tpu as pltpu
 from jax.sharding import PartitionSpec as P
 
-
-def body(factors, occ_energy, vir_energy, i_slot, j_slot, partner_device, pair_count):
+MESH = pl.DeviceIdType.MESH
+f32 = jnp.float32
+bf16 = jnp.bfloat16
+
+
+def slot_body(factors, occ_energy, vir_energy, i_slot, j_slot, partner_device, pair_count):
     held, virtuals, columns = factors.shape
     pair_slots = i_slot.shape[0]
     occ_count = lax.axis_size("occ")
@@ -95,6 +101,379 @@
     return (gamma, shared * factor_scale)
 
 
+def nt(a, b):
+    return lax.dot_general(a, b, (((1,), (1,)), ((), ())), preferred_element_type=f32)
+
+
+def tn(a, b):
+    return lax.dot_general(a, b, (((0,), (0,)), ((), ())), preferred_element_type=f32)
+
+
+def kernel(
+    f_ref, cnt_ref, e_ref, vcol_ref, vrow_ref,
+    gamma_ref, aux_ref,
+    kbuf, lbuf, kh, cnt, gacc, gsend, grecv, gfull, gsib, asend, arecv, tsend, trecv,
+    ky_s, ky_r, ksib_s, ksib_r, z_s, z_r, x_s, x_r, s_s, s_r,
+    cnt_s, cnt_r, g_s, g_r, gs_s, gs_r, a_s, a_r, t_s, t_r,
+):
+    occ_count = lax.axis_size("occ")
+    lines = occ_count // 2
+    held, virtuals, width = f_ref.shape
+    half = virtuals // 2
+    o = lax.axis_index("occ")
+    a = lax.axis_index("aux")
+    z, x = o // 2, o % 2
+    y, c = a // 2, a % 2
+    oy, oc, ox = 1 - y, 1 - c, 1 - x
+
+    def dev(occ, aux):
+        return {"occ": occ, "aux": aux}
+
+    y_peer, sibling = dev(o, oy * 2 + c), dev(o, y * 2 + oc)
+    x_peer = dev(z * 2 + ox, a)
+
+    def rcopy(src, dst, ss, rs, target):
+        return pltpu.make_async_remote_copy(
+            src_ref=src, dst_ref=dst, send_sem=ss, recv_sem=rs, device_id=target, device_id_type=MESH
+        )
+
+    barrier = pltpu.get_barrier_semaphore()
+    for s in range(1, occ_count):
+        pl.semaphore_signal(barrier, inc=1, device_id=dev((o + s) % occ_count, a), device_id_type=MESH)
+    pl.semaphore_signal(barrier, inc=1, device_id=y_peer, device_id_type=MESH)
+    pl.semaphore_signal(barrier, inc=1, device_id=sibling, device_id_type=MESH)
+    ta = o // 2
+    for h in range(2):
+        @pl.when(jnp.logical_or(ta != a, o != 2 * a + h))
+        def _():
+            pl.semaphore_signal(barrier, inc=1, device_id=dev(2 * a + h, ta), device_id_type=MESH)
+    pl.semaphore_wait(barrier, occ_count + 1 + jnp.where(ta != a, 2, 1))
+
+    def ky(r):
+        return rcopy(f_ref.at[r], kbuf.at[c, y, r], ky_s.at[r], ky_r.at[r], y_peer)
+
+    def ky_wait(r):
+        rcopy(f_ref.at[r], kbuf.at[c, oy, r], ky_s.at[r], ky_r.at[r], y_peer).wait_recv()
+
+    def ksib(n, yy, r):
+        return rcopy(kbuf.at[c, yy, r], kbuf.at[c, yy, r], ksib_s.at[n], ksib_r.at[n], sibling)
+
+    def ksib_wait(n, yy, r):
+        rcopy(kbuf.at[oc, yy, r], kbuf.at[oc, yy, r], ksib_s.at[n], ksib_r.at[n], sibling).wait_recv()
+
+    def item(oo, yy):
+        return lbuf.at[oo, c, yy]
+
+    def z_copy(d, zz, yy):
+        oo = zz * 2 + x
+        return rcopy(item(oo, yy), item(oo, yy), z_s.at[d, zz, yy], z_r.at[zz, yy], dev((z + 1 - 2 * d) * 2 + x, a))
+
+    def x_copy(zz, yy):
+        oo = zz * 2 + x
+        return rcopy(item(oo, yy), item(oo, yy), x_s.at[zz, yy], x_r.at[zz, yy], x_peer)
+
+    def x_wait(zz, yy):
+        oo = zz * 2 + ox
+        rcopy(item(oo, yy), item(oo, yy), x_s.at[zz, yy], x_r.at[zz, yy], x_peer).wait_recv()
+
+    def s_copy(oo, yy):
+        return rcopy(item(oo, yy), item(oo, yy), s_s.at[oo, yy], s_r.at[oo, yy], sibling)
+
+    def s_wait(oo, yy):
+        there = lbuf.at[oo, oc, yy]
+        rcopy(there, there, s_s.at[oo, yy], s_r.at[oo, yy], sibling).wait_recv()
+
+    def forward(zz, yy, right, left):
+        @pl.when(jnp.logical_and(right, z + 1 < lines))
+        def _():
+            z_copy(0, zz, yy).start()
+
+        @pl.when(jnp.logical_and(left, z > 0))
+        def _():
+            z_copy(1, zz, yy).start()
+
+        x_copy(zz, yy).start()
+        s_copy(zz * 2 + x, yy).start()
+
+    ky(oy).start()
+    lbuf[o, c, y] = f_ref[y]
+    forward(z, y, True, True)
+    ky(y).start()
+    kbuf[c, y] = f_ref[...]
+    ksib(0, y, 0).start()
+    ksib(1, y, 1).start()
+    cnt[o] = cnt_ref[...]
+
+    def cnt_copy(oo):
+        return rcopy(cnt_ref, cnt.at[o], cnt_s.at[oo], cnt_r.at[o], dev(oo, a))
+
+    for s in range(1, occ_count):
+        cnt_copy((o + s) % occ_count).start()
+
+    ky_wait(y)
+    lbuf[o, c, oy] = kbuf[c, oy, y]
+    forward(z, oy, True, True)
+    ksib(2, oy, y).start()
+    ky_wait(oy)
+    ksib(3, oy, oy).start()
+
+    gacc[...] = jnp.zeros_like(gacc)
+    for s in range(1, occ_count):
+        oo = (o + s) % occ_count
+        rcopy(cnt_ref, cnt.at[oo], cnt_s.at[oo], cnt_r.at[oo], dev(oo, a)).wait_recv()
+    ksib_wait(0, y, 0)
+    ksib_wait(1, y, 1)
+    ksib_wait(2, oy, y)
+    ksib_wait(3, oy, oy)
+    for cc in range(2):
+        for yy in range(2):
+            for k in range(2):
+                kh[cc, yy, k * half:(k + 1) * half] = kbuf[cc, yy, k, pl.ds(c * half, half)]
+    vhalf = vcol_ref[pl.ds(c * half, half)]
+    side = jnp.concatenate([vhalf - e_ref[2 * o], vhalf - e_ref[2 * o + 1]], axis=0)
+    vrow = vrow_ref[...]
+    rows8 = lax.broadcasted_iota(jnp.int32, cnt_ref.shape, 0)
+    lanes8 = lax.broadcasted_iota(jnp.int32, cnt_ref.shape, 1)
+
+    def pick(tile, row, lane):
+        here = jnp.logical_and(rows8 == row, lanes8 == lane)
+        return jnp.sum(jnp.where(here, tile, 0.0), keepdims=True)
+
+    def work(oo):
+        far = 2 * oo + y
+        inter = nt(kh[0, 0], lbuf[oo, 0, 0])
+        inter += nt(kh[0, 1], lbuf[oo, 0, 1])
+        inter += nt(kh[1, 0], lbuf[oo, 1, 0])
+        inter += nt(kh[1, 1], lbuf[oo, 1, 1])
+        amplitude = (inter / (side + (vrow - e_ref[far]))).astype(bf16)
+        mine, theirs = cnt[o], cnt[oo]
+        w1 = [pick(mine, k, far) for k in range(2)]
+        w2 = [pick(theirs, y, 2 * o + k) for k in range(2)]
+        for cc in range(2):
+            for yy in range(2):
+                term = jnp.dot(amplitude, lbuf[oo, cc, yy], preferred_element_type=f32)
+                for k in range(2):
+                    part = term[k * half:(k + 1) * half]
+                    gacc[cc, yy, k * half:(k + 1) * half] += (
+                        w1[k] * part + w2[k] * part.astype(bf16).astype(f32)
+                    )
+
+    def place(d, sign):
+        zz = z - d + 2 * d * sign
+        ok = jnp.logical_and(jnp.logical_and(zz >= 0, zz < lines), jnp.logical_or(d > 0, sign == 0))
+        return zz, ok
+
+    def step(d, carry):
+        @pl.when(d < lines)
+        def _():
+            for n in range(2):
+                yy = (y + n) % 2
+                for sign in range(2):
+                    zz, ok = place(d, sign)
+
+                    @pl.when(ok)
+                    def _():
+                        z_copy(0, zz, yy).wait_recv()
+                        forward(zz, yy, sign == 0, sign == 1)
+
+        before = d - 1
+        for sign in range(2):
+            zz, ok = place(before, sign)
+
+            @pl.when(ok)
+            def _():
+                for n in range(2):
+                    yy = (y + n) % 2
+                    x_wait(zz, yy)
+                    s_copy(zz * 2 + ox, yy).start()
+
+        def each(n, carry):
+            zz, ok = place(before, n // 2)
+            oo = zz * 2 + (x + n) % 2
+
+            @pl.when(ok)
+            def _():
+                s_wait(oo, 0)
+                s_wait(oo, 1)
+                work(oo)
+
+            return carry
+
+        lax.fori_loop(0, 4, each, 0)
+        return carry
+
+    lax.fori_loop(1, lines + 1, step, 0)
+
+    def g_copy(cc):
+        return rcopy(gsend.at[cc], grecv.at[cc], g_s.at[cc], g_r.at[cc], y_peer)
+
+    for n in range(2):
+        cc = (c + 1 + n) % 2
+        gsend[cc] = gacc[cc, oy].astype(bf16)
+        g_copy(cc).start()
+    for n in range(2):
+        cc = (c + 1 + n) % 2
+        g_copy(cc).wait_recv()
+        gfull[n] = gacc[cc, y] + grecv[cc].astype(f32)
+        if n == 0:
+            gs_copy = rcopy(gfull.at[0], gsib, gs_s, gs_r, sibling)
+            gs_copy.start()
+    for k in range(2):
+        gamma_ref[k, pl.ds(c * half, half)] = gfull[1, k * half:(k + 1) * half]
+    gs_copy.wait_recv()
+    for k in range(2):
+        gamma_ref[k, pl.ds(oc * half, half)] = gsib[k * half:(k + 1) * half]
+    rounded = gamma_ref[...].reshape(held * virtuals, width).astype(bf16)
+
+    out_width = aux_ref.shape[1]
+
+    def a_copy(oo):
+        return rcopy(asend.at[oo], arecv.at[o], a_s.at[oo], a_r.at[o], dev(oo, a))
+
+    for n in range(4):
+        block = (ta + n) % 4
+        terms = tn(rounded, kbuf[block % 2, block // 2].reshape(held * virtuals, width))
+        for h in range(2):
+            oo = 2 * block + h
+            part = terms[:, h * out_width:(h + 1) * out_width]
+            asend[oo] = part.astype(bf16)
+
+            @pl.when(oo == o)
+            def _():
+                aux_ref[...] = part
+
+            @pl.when(oo != o)
+            def _():
+                a_copy(oo).start()
+
+    total = aux_ref[...]
+    for s in range(1, occ_count):
+        oo = (o + s) % occ_count
+        rcopy(asend.at[oo], arecv.at[oo], a_s.at[oo], a_r.at[oo], dev(oo, a)).wait_recv()
+        total += arecv[oo].astype(f32)
+    for h in range(2):
+        tsend[h] = total[h * out_width:(h + 1) * out_width]
+
+    def t_copy(h):
+        return rcopy(tsend.at[h], trecv.at[o % 2], t_s.at[h], t_r.at[o % 2], dev(2 * a + h, ta))
+
+    for h in range(2):
+        far = jnp.logical_or(ta != a, o != 2 * a + h)
+
+        @pl.when(far)
+        def _():
+            t_copy(h).start()
+
+        @pl.when(jnp.logical_not(far))
+        def _():
+            trecv[o % 2] = tsend[h]
+
+    scale = float(occ_count * held * virtuals) ** (-0.5)
+    for h in range(2):
+        @pl.when(jnp.logical_or(ta != a, o != 2 * a + h))
+        def _():
+            rcopy(tsend.at[h], trecv.at[h], t_s.at[h], t_r.at[h], dev(2 * a + h, ta)).wait_recv()
+
+        rows = slice(h * out_width, (h + 1) * out_width)
+        aux_ref[rows] = (total[rows] + trecv[h].T) * scale
+
+    for r in range(2):
+        ky(r).wait_send()
+        g_copy(r).wait_send()
+    ksib(0, y, 0).wait_send()
+    ksib(1, y, 1).wait_send()
+    ksib(2, oy, y).wait_send()
+    ksib(3, oy, oy).wait_send()
+    gs_copy.wait_send()
+    for s in range(1, occ_count):
+        oo = (o + s) % occ_count
+        cnt_copy(oo).wait_send()
+        a_copy(oo).wait_send()
+    for h in range(2):
+        @pl.when(jnp.logical_or(ta != a, o != 2 * a + h))
+        def _():
+            t_copy(h).wait_send()
+
+    def drain(zz, carry):
+        for yy in range(2):
+            @pl.when(jnp.logical_and(zz <= z, z + 1 < lines))
+            def _():
+                z_copy(0, zz, yy).wait_send()
+
+            @pl.when(jnp.logical_and(zz >= z, z > 0))
+            def _():
+                z_copy(1, zz, yy).wait_send()
+
+            x_copy(zz, yy).wait_send()
+            s_copy(zz * 2, yy).wait_send()
+            s_copy(zz * 2 + 1, yy).wait_send()
+        return carry
+
+    lax.fori_loop(0, lines, drain, 0)
+
+
+def table_body(factors, occ_energy, vir_energy, i_slot, j_slot, partner_device, pair_count):
+    held, virtuals, width = factors.shape
+    slots = i_slot.shape[0]
+    occ_count = lax.axis_size("occ")
+    lines = occ_count // 2
+    out_width = 4 * width // occ_count
+    living = jnp.arange(slots, dtype=jnp.int32) < pair_count[0]
+    far = partner_device[:, 0] * held + j_slot
+    row_hit = jnp.logical_and(
+        i_slot[None, :, None] == jnp.arange(8, dtype=jnp.int32)[:, None, None], living[None, :, None]
+    )
+    col_hit = far[None, :, None] == jnp.arange(128, dtype=jnp.int32)[None, None, :]
+    counts = jnp.sum(jnp.logical_and(row_hit, col_hit).astype(f32), axis=1)
+    vmem = pl.BlockSpec(memory_space=pltpu.VMEM)
+    dma = pltpu.SemaphoreType.DMA
+    return pl.pallas_call(
+        kernel,
+        out_shape=(
+            jax.ShapeDtypeStruct((held, virtuals, width), f32),
+            jax.ShapeDtypeStruct((width, out_width), f32),
+        ),
+        in_specs=[vmem, vmem, pl.BlockSpec(memory_space=pltpu.SMEM), vmem, vmem],
+        out_specs=(vmem, vmem),
+        scratch_shapes=[
+            pltpu.VMEM((2, 2, held, virtuals, width), bf16),
+            pltpu.VMEM((occ_count, 2, 2, virtuals, width), bf16),
+            pltpu.VMEM((2, 2, virtuals, width), bf16),
+            pltpu.VMEM((occ_count, 8, 128), f32),
+            pltpu.VMEM((2, 2, virtuals, width), f32),
+            pltpu.VMEM((2, virtuals, width), bf16),
+            pltpu.VMEM((2, virtuals, width), bf16),
+            pltpu.VMEM((2, virtuals, width), f32),
+            pltpu.VMEM((virtuals, width), f32),
+            pltpu.VMEM((occ_count, width, out_width), bf16),
+            pltpu.VMEM((occ_count, width, out_width), bf16),
+            pltpu.VMEM((2, out_width, out_width), f32),
+            pltpu.VMEM((2, out_width, out_width), f32),
+            dma((2,)), dma((2,)), dma((4,)), dma((4,)),
+            dma((2, lines, 2)), dma((lines, 2)), dma((lines, 2)), dma((lines, 2)),
+            dma((occ_count, 2)), dma((occ_count, 2)),
+            dma((occ_count,)), dma((occ_count,)), dma((2,)), dma((2,)), dma, dma,
+            dma((occ_count,)), dma((occ_count,)), dma((2,)), dma((2,)),
+        ],
+        compiler_params=pltpu.CompilerParams(
+            collective_id=0, has_side_effects=True, vmem_limit_bytes=40 * 1024 * 1024
+        ),
+    )(factors, counts, occ_energy, vir_energy[:, None], vir_energy[None, :])
+
+
+def body(*operands):
+    factors, i_slot = operands[0], operands[3]
+    held, virtuals, width = factors.shape
+    occ_count, aux_count = lax.axis_size("occ"), lax.axis_size("aux")
+    orbitals = held * occ_count
+    fits = (
+        held == 2 and aux_count == 4 and occ_count == 2 * aux_count and orbitals <= 128
+        and orbitals * orbitals <= occ_count * i_slot.shape[0]
+        and virtuals == width and width % 256 == 0
+    )
+    return table_body(*operands) if fits else slot_body(*operands)
+
+
 def solution(mesh):
     placed = (P("occ", None, "aux"), P(), P(), P("occ"), P("occ"), P("occ", None), P("occ"))
     return jax.shard_map(

time: 499 us -> 70.8 us (0.14)
  waiting for transfers between devices: 405 us -> 0 us
  Pallas kernels: 0 us -> 63.2 us
  matrix products: 33.3 us -> 0 us
  local copies, waits for them, and re-layouts: 22.4 us -> 4.91 us
  between operations: 14.6 us -> 1.32 us
  starting transfers between devices: 10.8 us -> 0 us
  other arithmetic: 9.44 us -> 0.2 us
    psum x1 -> x0, waiting for transfers between devices: 147 us -> none  [body(): summed = lax.psum(partial_value, 'aux')]
    all_to_all x2 -> x0, waiting for transfers between devices: 128 us -> none  [the longest x1 128 us: body(): lax.all_to_all(placed, 'occ', split_axis=0, concat_axis=0, tiled=True)]
    all_gather x2 -> x0, waiting for transfers between devices: 69 us -> none  [the longest x1 46.3 us: body(): piece = lax.all_gather(factors, 'occ', axis=0, tiled=True)]
    pallas_call x0 -> x1, Pallas kernels: none -> 63.2 us  [table_body(): pl.pallas_call(kernel, out_shape=(jax.ShapeDtypeStruct((held, virtuals, w...]
    reduce_scatter x1 -> x0, waiting for transfers between devices: 60.6 us -> none  [body(): shared = lax.psum_scatter(terms, 'occ', scatter_dimension=1, tiled=True)]
    dot_general x9 -> x0, matrix products: 33.3 us -> none  [the longest x1 7.98 us: body(): jnp.einsum('po,pvq->ovq', owner_hit, local_terms, precision=lax.Precision...]
    all_to_all x2 -> x0, starting transfers between devices: 10.7 us -> none  [the longest x1 5.64 us: body(): lax.all_to_all(placed, 'occ', split_axis=0, concat_axis=0, tiled=True)]
    unnamed x28 -> x14, local copies, waits for them, and re-layouts: 14.2 us -> 4.78 us
  transfers between devices with their start and end apart: 6 -> 0, of which waited for: 5 -> 0; matrix products, arithmetic and copies ran while one was open for 6% -> 0% of each run, Pallas kernels for 0% -> 0%
where the time goes in v1:
time: 70.8 us; the launch traced here: 69.7 us
  Pallas kernels  63.2 us (89%)
  local copies, waits for them, and re-layouts  4.91 us (7%)
  between operations  1.32 us (2%)
    pallas_call x1, Pallas kernels, table_body(): pl.pallas_call(kernel, out_shape=(jax.ShapeDtypeStruct((held, virtuals, w...  63.2 us
    unnamed x14, local copies, waits for them, and re-layouts  4.78 us

profile of v1, /device:TPU:3, one launch (start us, length us, event | category | flops | bytes accessed | tf_op | source)
XLA Modules:
  0.0 69.7 jit_solution(7880225683603116045)
XLA Ops:
  1.3 0.0 copy-start.3
  1.3 0.6 copy-done.3
  1.9 0.0 copy-start.4
  1.9 0.0 copy-start.5
  1.9 0.6 copy-done.4
  2.6 0.0 copy-done.5
  2.6 0.1 iota_compare_fusion
  2.7 0.0 copy-start.1
  2.7 0.1 convert_reduce_fusion.cnt_ref
  2.8 0.6 copy-done.1
  3.4 0.0 copy-start.2
  3.4 0.1 copy.10.vcol_ref
  3.5 0.5 copy-done.2
  4.0 0.0 copy-start
  4.0 0.9 %copy-done = bf16[2,256,256]{2,1,0:T(8,128)(2,1)S(1)} copy-done((bf16[2,256,256]{2,1,0:T(8,128)(2,1)S(1)}, bf16[2,256,256]{2,1,0:T(8,128)(2,1)}, u32[]{:S(2)}) %copy-start) | copy-done | bytes 262168
  5.0 63.2 %shard_map.86 = (f32[2,256,256]{2,1,0:T(8,128)S(1)}, f32[256,128]{1,0:T(8,128)S(1)}) custom-call(bf16[2,256,256]{2,1,0:T(8,128)(2,1)S(1)} %copy-done, f32[8,128]{1,0:T(8,128)S(1)} %convert_reduce_fusion.cnt_ref, f32[16]{0:T(128)S(1)} %copy-done.2, f32[256,1]{1,0:T(8,128)S(1)} %copy.10.vcol_ref, f32[1,256]{1,0:T(1,128)S(1)} %bitcast.7), custom_call_target="tpu_custom_call" | custom-call | tf_op jit(solution)/shard_map/pallas_call | solution.py:430
  68.2 0.8 %copy.14 = f32[2,256,256]{2,1,0:T(8,128)} copy(f32[2,256,256]{2,1,0:T(8,128)S(1)} %get-tuple-element.4) | data formatting | bytes 1048576
  69.0 0.7 copy.15
  (3 shorter events, 0.0 us)
Async XLA Ops:
  1.3 0.7 copy-start.3
  1.9 0.7 copy-start.4
  1.9 0.7 copy-start.5
  2.7 0.7 copy-start.1
  3.4 0.7 copy-start.2
  4.0 0.9 %copy-start = (bf16[2,256,256]{2,1,0:T(8,128)(2,1)S(1)}, bf16[2,256,256]{2,1,0:T(8,128)(2,1)}, u32[]{:S(2)}) copy-start(bf16[2,256,256]{2,1,0:T(8,128)(2,1)} %f_ref.1) | copy-start | bytes 786436

commit v2 on v1

--- a/solution.py
+++ b/solution.py
@@ -304,93 +304,101 @@
 
     lax.fori_loop(1, lines + 1, step, 0)
 
-    def g_copy(cc):
-        return rcopy(gsend.at[cc], grecv.at[cc], g_s.at[cc], g_r.at[cc], y_peer)
-
-    for n in range(2):
-        cc = (c + 1 + n) % 2
-        gsend[cc] = gacc[cc, oy].astype(bf16)
-        g_copy(cc).start()
-    for n in range(2):
-        cc = (c + 1 + n) % 2
-        g_copy(cc).wait_recv()
-        gfull[n] = gacc[cc, y] + grecv[cc].astype(f32)
-        if n == 0:
-            gs_copy = rcopy(gfull.at[0], gsib, gs_s, gs_r, sibling)
-            gs_copy.start()
-    for k in range(2):
-        gamma_ref[k, pl.ds(c * half, half)] = gfull[1, k * half:(k + 1) * half]
-    gs_copy.wait_recv()
-    for k in range(2):
-        gamma_ref[k, pl.ds(oc * half, half)] = gsib[k * half:(k + 1) * half]
-    rounded = gamma_ref[...].reshape(held * virtuals, width).astype(bf16)
-
     out_width = aux_ref.shape[1]
 
-    def a_copy(oo):
-        return rcopy(asend.at[oo], arecv.at[o], a_s.at[oo], a_r.at[o], dev(oo, a))
-
-    for n in range(4):
-        block = (ta + n) % 4
-        terms = tn(rounded, kbuf[block % 2, block // 2].reshape(held * virtuals, width))
-        for h in range(2):
-            oo = 2 * block + h
-            part = terms[:, h * out_width:(h + 1) * out_width]
-            asend[oo] = part.astype(bf16)
-
-            @pl.when(oo == o)
-            def _():
-                aux_ref[...] = part
-
-            @pl.when(oo != o)
-            def _():
-                a_copy(oo).start()
-
-    total = aux_ref[...]
-    for s in range(1, occ_count):
-        oo = (o + s) % occ_count
-        rcopy(asend.at[oo], arecv.at[oo], a_s.at[oo], a_r.at[oo], dev(oo, a)).wait_recv()
-        total += arecv[oo].astype(f32)
-    for h in range(2):
-        tsend[h] = total[h * out_width:(h + 1) * out_width]
+    def cols(h):
+        return slice(h * out_width, (h + 1) * out_width)
+
+    def g_copy(h, cc):
+        return rcopy(gsend.at[h, cc], grecv.at[h, cc], g_s.at[h, cc], g_r.at[h, cc], y_peer)
+
+    def gs_copy(h):
+        return rcopy(gfull.at[h], gsib.at[h], gs_s.at[h], gs_r.at[h], sibling)
+
+    def a_copy(h, oo):
+        return rcopy(asend.at[h, oo], arecv.at[h, o], a_s.at[h, oo], a_r.at[h, o], dev(oo, a))
 
     def t_copy(h):
         return rcopy(tsend.at[h], trecv.at[o % 2], t_s.at[h], t_r.at[o % 2], dev(2 * a + h, ta))
 
-    for h in range(2):
-        far = jnp.logical_or(ta != a, o != 2 * a + h)
-
-        @pl.when(far)
+    def t_far(h):
+        return jnp.logical_or(ta != a, o != 2 * a + h)
+
+    for h in range(2):
+        for n in range(2):
+            cc = (c + 1 + n) % 2
+            gsend[h, cc] = gacc[cc, oy][:, cols(h)].astype(bf16)
+            g_copy(h, cc).start()
+
+    for h in range(2):
+        g_copy(h, oc).wait_recv()
+        gfull[h] = gacc[oc, y][:, cols(h)] + grecv[h, oc].astype(f32)
+        gs_copy(h).start()
+        g_copy(h, c).wait_recv()
+        mine = gacc[c, y][:, cols(h)] + grecv[h, c].astype(f32)
+        for k in range(2):
+            gamma_ref[k, pl.ds(c * half, half), cols(h)] = mine[k * half:(k + 1) * half]
+        gs_copy(h).wait_recv()
+        for k in range(2):
+            gamma_ref[k, pl.ds(oc * half, half), cols(h)] = gsib[h, k * half:(k + 1) * half]
+        rounded = gamma_ref[:, :, cols(h)].reshape(held * virtuals, out_width).astype(bf16)
+
+        for n in range(4):
+            block = (ta + 2 + n) % 4
+            terms = tn(rounded, kbuf[block % 2, block // 2].reshape(held * virtuals, width))
+            for g in range(2):
+                oo = 2 * block + g
+                part = terms[:, cols(g)]
+                asend[h, oo] = part.astype(bf16)
+
+                @pl.when(oo == o)
+                def _():
+                    aux_ref[cols(h)] = part
+
+                @pl.when(oo != o)
+                def _():
+                    a_copy(h, oo).start()
+
+    for h in range(2):
+        total = aux_ref[cols(h)]
+        for s in range(1, occ_count):
+            oo = (o + s) % occ_count
+            rcopy(asend.at[h, oo], arecv.at[h, oo], a_s.at[h, oo], a_r.at[h, oo], dev(oo, a)).wait_recv()
+            total += arecv[h, oo].astype(f32)
+        tsend[h] = total
+
+        @pl.when(t_far(h))
         def _():
             t_copy(h).start()
 
-        @pl.when(jnp.logical_not(far))
+        @pl.when(jnp.logical_not(t_far(h)))
         def _():
             trecv[o % 2] = tsend[h]
 
     scale = float(occ_count * held * virtuals) ** (-0.5)
     for h in range(2):
-        @pl.when(jnp.logical_or(ta != a, o != 2 * a + h))
+        @pl.when(t_far(h))
         def _():
             rcopy(tsend.at[h], trecv.at[h], t_s.at[h], t_r.at[h], dev(2 * a + h, ta)).wait_recv()
 
-        rows = slice(h * out_width, (h + 1) * out_width)
-        aux_ref[rows] = (total[rows] + trecv[h].T) * scale
+        aux_ref[cols(h)] = (tsend[h] + trecv[h].T) * scale
 
     for r in range(2):
         ky(r).wait_send()
-        g_copy(r).wait_send()
+        g_copy(r, 0).wait_send()
+        g_copy(r, 1).wait_send()
+        gs_copy(r).wait_send()
     ksib(0, y, 0).wait_send()
     ksib(1, y, 1).wait_send()
     ksib(2, oy, y).wait_send()
     ksib(3, oy, oy).wait_send()
-    gs_copy.wait_send()
     for s in range(1, occ_count):
         oo = (o + s) % occ_count
         cnt_copy(oo).wait_send()
-        a_copy(oo).wait_send()
-    for h in range(2):
-        @pl.when(jnp.logical_or(ta != a, o != 2 * a + h))
+        a_copy(0, oo).wait_send()
+        a_copy(1, oo).wait_send()
+    for h in range(2):
+        @pl.when(t_far(h))
         def _():
             t_copy(h).wait_send()
 
@@ -441,19 +449,19 @@
             pltpu.VMEM((2, 2, virtuals, width), bf16),
             pltpu.VMEM((occ_count, 8, 128), f32),
             pltpu.VMEM((2, 2, virtuals, width), f32),
-            pltpu.VMEM((2, virtuals, width), bf16),
-            pltpu.VMEM((2, virtuals, width), bf16),
-            pltpu.VMEM((2, virtuals, width), f32),
-            pltpu.VMEM((virtuals, width), f32),
-            pltpu.VMEM((occ_count, width, out_width), bf16),
-            pltpu.VMEM((occ_count, width, out_width), bf16),
+            pltpu.VMEM((2, 2, virtuals, out_width), bf16),
+            pltpu.VMEM((2, 2, virtuals, out_width), bf16),
+            pltpu.VMEM((2, virtuals, out_width), f32),
+            pltpu.VMEM((2, virtuals, out_width), f32),
+            pltpu.VMEM((2, occ_count, out_width, out_width), bf16),
+            pltpu.VMEM((2, occ_count, out_width, out_width), bf16),
             pltpu.VMEM((2, out_width, out_width), f32),
             pltpu.VMEM((2, out_width, out_width), f32),
             dma((2,)), dma((2,)), dma((4,)), dma((4,)),
             dma((2, lines, 2)), dma((lines, 2)), dma((lines, 2)), dma((lines, 2)),
             dma((occ_count, 2)), dma((occ_count, 2)),
-            dma((occ_count,)), dma((occ_count,)), dma((2,)), dma((2,)), dma, dma,
-            dma((occ_count,)), dma((occ_count,)), dma((2,)), dma((2,)),
+            dma((occ_count,)), dma((occ_count,)), dma((2, 2)), dma((2, 2)), dma((2,)), dma((2,)),
+            dma((2, occ_count)), dma((2, occ_count)), dma((2,)), dma((2,)),
         ],
         compiler_params=pltpu.CompilerParams(
             collective_id=0, has_side_effects=True, vmem_limit_bytes=40 * 1024 * 1024
@@ -469,7 +477,7 @@
     fits = (
         held == 2 and aux_count == 4 and occ_count == 2 * aux_count and orbitals <= 128
         and orbitals * orbitals <= occ_count * i_slot.shape[0]
-        and virtuals == width and width % 256 == 0
+        and virtuals == width and width % 256 == 0 and 4 * width == occ_count * 128
     )
     return table_body(*operands) if fits else slot_body(*operands)
 

time: 70.8 us -> 66.7 us (0.942); the launches traced: 69.7 us -> 66.5 us
  Pallas kernels: 63.2 us -> 60 us
    pallas_call x1, Pallas kernels: 63.2 us -> 60 us  [table_body(): pl.pallas_call(kernel, out_shape=(jax.ShapeDtypeStruct((held, virtuals, w...]
where the time goes in v2:
time: 66.7 us; the launch traced here: 66.5 us
  Pallas kernels  60 us (90%)
  local copies, waits for them, and re-layouts  4.91 us (7%)
  between operations  1.32 us (2%)
    pallas_call x1, Pallas kernels, table_body(): pl.pallas_call(kernel, out_shape=(jax.ShapeDtypeStruct((held, virtuals, w...  60 us
    unnamed x14, local copies, waits for them, and re-layouts  4.78 us

profile of v2, /device:TPU:3, one launch (start us, length us, event | category | flops | bytes accessed | tf_op | source)
XLA Modules:
  0.0 66.5 jit_solution(8800370073092115350)
XLA Ops:
  1.3 0.0 copy-start.3
  1.3 0.6 copy-done.3
  1.9 0.0 copy-start.4
  1.9 0.0 copy-start.5
  1.9 0.6 copy-done.4
  2.6 0.0 copy-done.5
  2.6 0.1 iota_compare_fusion
  2.7 0.0 copy-start.1
  2.7 0.1 convert_reduce_fusion.cnt_ref
  2.8 0.6 copy-done.1
  3.4 0.0 copy-start.2
  3.4 0.1 copy.10.vcol_ref
  3.5 0.5 copy-done.2
  4.0 0.0 copy-start
  4.0 0.9 %copy-done = bf16[2,256,256]{2,1,0:T(8,128)(2,1)S(1)} copy-done((bf16[2,256,256]{2,1,0:T(8,128)(2,1)S(1)}, bf16[2,256,256]{2,1,0:T(8,128)(2,1)}, u32[]{:S(2)}) %copy-start) | copy-done | bytes 262168
  5.0 60.0 %shard_map.86 = (f32[2,256,256]{2,1,0:T(8,128)S(1)}, f32[256,128]{1,0:T(8,128)S(1)}) custom-call(bf16[2,256,256]{2,1,0:T(8,128)(2,1)S(1)} %copy-done, f32[8,128]{1,0:T(8,128)S(1)} %convert_reduce_fusion.cnt_ref, f32[16]{0:T(128)S(1)} %copy-done.2, f32[256,1]{1,0:T(8,128)S(1)} %copy.10.vcol_ref, f32[1,256]{1,0:T(1,128)S(1)} %bitcast.7), custom_call_target="tpu_custom_call" | custom-call | tf_op jit(solution)/shard_map/pallas_call | solution.py:438
  65.0 0.8 %copy.14 = f32[2,256,256]{2,1,0:T(8,128)} copy(f32[2,256,256]{2,1,0:T(8,128)S(1)} %get-tuple-element.4) | data formatting | bytes 1048576
  65.8 0.7 copy.15
  (3 shorter events, 0.0 us)
Async XLA Ops:
  1.3 0.7 copy-start.3
  1.9 0.7 copy-start.4
  1.9 0.7 %copy-start.5 = (s32[32,1]{0,1:T(1,128)S(1)}, s32[32,1]{0,1:T(1,128)}, u32[]{:S(2)}) copy-start(s32[32,1]{0,1:T(1,128)} %param.12) | copy-start | bytes 388
  2.7 0.7 %copy-start.1 = (f32[256]{0:T(256)S(1)}, f32[256]{0:T(256)}, u32[]{:S(2)}) copy-start(f32[256]{0:T(256)} %param.9) | copy-start | bytes 3076
  3.4 0.7 copy-start.2
  4.0 0.9 %copy-start = (bf16[2,256,256]{2,1,0:T(8,128)(2,1)S(1)}, bf16[2,256,256]{2,1,0:T(8,128)(2,1)}, u32[]{:S(2)}) copy-start(bf16[2,256,256]{2,1,0:T(8,128)(2,1)} %f_ref.1) | copy-start | bytes 786436

commit v3 on v2

--- a/solution.py
+++ b/solution.py
@@ -110,11 +110,12 @@
 
 
 def kernel(
-    f_ref, cnt_ref, e_ref, vcol_ref, vrow_ref,
+    f_hbm, e_hbm, v_hbm, i_hbm, j_hbm, partner_hbm, count_ref,
     gamma_ref, aux_ref,
     kbuf, lbuf, kh, cnt, gacc, gsend, grecv, gfull, gsib, asend, arecv, tsend, trecv,
     ky_s, ky_r, ksib_s, ksib_r, z_s, z_r, x_s, x_r, s_s, s_r,
     cnt_s, cnt_r, g_s, g_r, gs_s, gs_r, a_s, a_r, t_s, t_r,
+    f_ref, e_ref, v_ref, i_ref, j_ref, partner_ref, cnt_ref, side, in_s,
 ):
     occ_count = lax.axis_size("occ")
     lines = occ_count // 2
@@ -137,6 +138,14 @@
             src_ref=src, dst_ref=dst, send_sem=ss, recv_sem=rs, device_id=target, device_id_type=MESH
         )
 
+    pairs = (
+        (f_hbm, f_ref), (e_hbm, e_ref), (v_hbm, v_ref), (i_hbm, i_ref), (j_hbm, j_ref),
+        (partner_hbm, partner_ref),
+    )
+    loads = [pltpu.make_async_copy(there, here, in_s.at[n]) for n, (there, here) in enumerate(pairs)]
+    for load in loads:
+        load.start()
+
     barrier = pltpu.get_barrier_semaphore()
     for s in range(1, occ_count):
         pl.semaphore_signal(barrier, inc=1, device_id=dev((o + s) % occ_count, a), device_id_type=MESH)
@@ -195,6 +204,7 @@
         x_copy(zz, yy).start()
         s_copy(zz * 2 + x, yy).start()
 
+    loads[0].wait()
     ky(oy).start()
     lbuf[o, c, y] = f_ref[y]
     forward(z, y, True, True)
@@ -202,6 +212,16 @@
     kbuf[c, y] = f_ref[...]
     ksib(0, y, 0).start()
     ksib(1, y, 1).start()
+    for load in loads[1:]:
+        load.wait()
+
+    slots = i_ref.shape[1]
+    order = lax.broadcasted_iota(jnp.int32, (8, slots), 1)
+    row_hit = jnp.logical_and(
+        i_ref[...] == lax.broadcasted_iota(jnp.int32, (8, slots), 0), order < count_ref[0]
+    )
+    col_hit = partner_ref[...] * held + j_ref[...] == lax.broadcasted_iota(jnp.int32, (128, slots), 0)
+    cnt_ref[...] = nt(row_hit.astype(f32).astype(bf16), col_hit.astype(f32).astype(bf16))
     cnt[o] = cnt_ref[...]
 
     def cnt_copy(oo):
@@ -229,9 +249,10 @@
         for yy in range(2):
             for k in range(2):
                 kh[cc, yy, k * half:(k + 1) * half] = kbuf[cc, yy, k, pl.ds(c * half, half)]
-    vhalf = vcol_ref[pl.ds(c * half, half)]
-    side = jnp.concatenate([vhalf - e_ref[2 * o], vhalf - e_ref[2 * o + 1]], axis=0)
-    vrow = vrow_ref[...]
+    column = jnp.broadcast_to(v_ref[:, pl.ds(pl.multiple_of(c * half, half), half)], (width, half)).T
+    side[0:half] = column - e_ref[0, 2 * o]
+    side[half:virtuals] = column - e_ref[0, 2 * o + 1]
+    vrow = v_ref[...]
     rows8 = lax.broadcasted_iota(jnp.int32, cnt_ref.shape, 0)
     lanes8 = lax.broadcasted_iota(jnp.int32, cnt_ref.shape, 1)
 
@@ -245,7 +266,7 @@
         inter += nt(kh[0, 1], lbuf[oo, 0, 1])
         inter += nt(kh[1, 0], lbuf[oo, 1, 0])
         inter += nt(kh[1, 1], lbuf[oo, 1, 1])
-        amplitude = (inter / (side + (vrow - e_ref[far]))).astype(bf16)
+        amplitude = (inter / (side[...] + (vrow - e_ref[0, far]))).astype(bf16)
         mine, theirs = cnt[o], cnt[oo]
         w1 = [pick(mine, k, far) for k in range(2)]
         w2 = [pick(theirs, y, 2 * o + k) for k in range(2)]
@@ -423,16 +444,10 @@
 def table_body(factors, occ_energy, vir_energy, i_slot, j_slot, partner_device, pair_count):
     held, virtuals, width = factors.shape
     slots = i_slot.shape[0]
+    orbitals = occ_energy.shape[0]
     occ_count = lax.axis_size("occ")
     lines = occ_count // 2
     out_width = 4 * width // occ_count
-    living = jnp.arange(slots, dtype=jnp.int32) < pair_count[0]
-    far = partner_device[:, 0] * held + j_slot
-    row_hit = jnp.logical_and(
-        i_slot[None, :, None] == jnp.arange(8, dtype=jnp.int32)[:, None, None], living[None, :, None]
-    )
-    col_hit = far[None, :, None] == jnp.arange(128, dtype=jnp.int32)[None, None, :]
-    counts = jnp.sum(jnp.logical_and(row_hit, col_hit).astype(f32), axis=1)
     vmem = pl.BlockSpec(memory_space=pltpu.VMEM)
     dma = pltpu.SemaphoreType.DMA
     return pl.pallas_call(
@@ -441,7 +456,7 @@
             jax.ShapeDtypeStruct((held, virtuals, width), f32),
             jax.ShapeDtypeStruct((width, out_width), f32),
         ),
-        in_specs=[vmem, vmem, pl.BlockSpec(memory_space=pltpu.SMEM), vmem, vmem],
+        in_specs=[pl.BlockSpec(memory_space=pltpu.HBM)] * 6 + [pl.BlockSpec(memory_space=pltpu.SMEM)],
         out_specs=(vmem, vmem),
         scratch_shapes=[
             pltpu.VMEM((2, 2, held, virtuals, width), bf16),
@@ -462,11 +477,23 @@
             dma((occ_count, 2)), dma((occ_count, 2)),
             dma((occ_count,)), dma((occ_count,)), dma((2, 2)), dma((2, 2)), dma((2,)), dma((2,)),
             dma((2, occ_count)), dma((2, occ_count)), dma((2,)), dma((2,)),
+            pltpu.VMEM((held, virtuals, width), bf16),
+            pltpu.SMEM((1, orbitals), f32),
+            pltpu.VMEM((1, virtuals), f32),
+            pltpu.VMEM((1, slots), jnp.int32),
+            pltpu.VMEM((1, slots), jnp.int32),
+            pltpu.VMEM((1, slots), jnp.int32),
+            pltpu.VMEM((8, 128), f32),
+            pltpu.VMEM((virtuals, virtuals), f32),
+            dma((6,)),
         ],
         compiler_params=pltpu.CompilerParams(
-            collective_id=0, has_side_effects=True, vmem_limit_bytes=40 * 1024 * 1024
+            collective_id=0, has_side_effects=True, vmem_limit_bytes=64 * 1024 * 1024
         ),
-    )(factors, counts, occ_energy, vir_energy[:, None], vir_energy[None, :])
+    )(
+        factors, occ_energy[None, :], vir_energy[None, :], i_slot[None, :], j_slot[None, :],
+        partner_device.reshape(1, slots), pair_count,
+    )
 
 
 def body(*operands):

time: 66.7 us -> 64.5 us (0.967)
  local copies, waits for them, and re-layouts: 4.91 us -> 2.56 us
    unnamed x14 -> x4, local copies, waits for them, and re-layouts: 4.78 us -> 2.56 us
where the time goes in v3:
time: 64.5 us; the launch traced here: 64.4 us
  Pallas kernels  60.5 us (94%)
  local copies, waits for them, and re-layouts  2.56 us (4%)
  between operations  1.3 us (2%)
    pallas_call x1, Pallas kernels, table_body(): pl.pallas_call(kernel, out_shape=(jax.ShapeDtypeStruct((held, virtuals, w...  60.5 us
    unnamed x4, local copies, waits for them, and re-layouts  2.56 us

profile of v3, /device:TPU:3, one launch (start us, length us, event | category | flops | bytes accessed | tf_op | source)
XLA Modules:
  0.0 64.4 jit_solution(13391556511810163834)
XLA Ops:
  1.3 60.5 %shard_map.86 = (f32[2,256,256]{2,1,0:T(8,128)}, f32[256,128]{1,0:T(8,128)}) custom-call(bf16[2,256,256]{2,1,0:T(8,128)(2,1)} %f_hbm.1, f32[1,16]{1,0:T(1,128)} %bitcast.6, f32[1,256]{1,0:T(1,128)} %bitcast.5, s32[1,32]{1,0:T(1,128)} %bitcast.7, s32[1,32]{1,0:T(1,128)} %bitcast.8, s32[1,32]{1,0:T(1,128)} %bitcast.9, s32[1]{0:T(128)S(6)} %copy.11.count_ref), custom_call_target="tpu_custom_call" | custom-call | tf_op jit(solution)/shard_map/pallas_call | solution.py:453
  61.8 0.0 copy-start
  61.8 1.9 %copy.12 = f32[2,256,256]{2,1,0:T(8,128)} copy(f32[2,256,256]{2,1,0:T(8,128)} %get-tuple-element.4) | data formatting | bytes 1048576
  63.7 0.0 copy-done
  63.7 0.7 %copy.13 = f32[256,128]{1,0:T(8,128)} copy(f32[256,128]{1,0:T(8,128)S(1)} %copy-done) | data formatting | bytes 262144
Async XLA Ops:
  61.8 1.9 %copy-start = (f32[256,128]{1,0:T(8,128)S(1)}, f32[256,128]{1,0:T(8,128)}, u32[]{:S(2)}) copy-start(f32[256,128]{1,0:T(8,128)} %get-tuple-element.5) | copy-start | bytes 393220

commit v4 on v3

--- a/solution.py
+++ b/solution.py
@@ -204,6 +204,31 @@
         x_copy(zz, yy).start()
         s_copy(zz * 2 + x, yy).start()
 
+    def place(d, sign):
+        zz = z - d + 2 * d * sign
+        ok = jnp.logical_and(jnp.logical_and(zz >= 0, zz < lines), jnp.logical_or(d > 0, sign == 0))
+        return zz, ok
+
+    def stage(d, n):
+        yy = (y + n) % 2
+        for sign in range(2):
+            zz, ok = place(d, sign)
+
+            @pl.when(ok)
+            def _():
+                z_copy(0, zz, yy).wait_recv()
+                forward(zz, yy, sign == 0, sign == 1)
+
+    def across(d, n):
+        yy = (y + n) % 2
+        for sign in range(2):
+            zz, ok = place(d, sign)
+
+            @pl.when(ok)
+            def _():
+                x_wait(zz, yy)
+                s_copy(zz * 2 + ox, yy).start()
+
     loads[0].wait()
     ky(oy).start()
     lbuf[o, c, y] = f_ref[y]
@@ -234,8 +259,12 @@
     lbuf[o, c, oy] = kbuf[c, oy, y]
     forward(z, oy, True, True)
     ksib(2, oy, y).start()
+    stage(1, 0)
+    across(0, 0)
     ky_wait(oy)
     ksib(3, oy, oy).start()
+    stage(1, 1)
+    across(0, 1)
 
     gacc[...] = jnp.zeros_like(gacc)
     for s in range(1, occ_count):
@@ -249,9 +278,9 @@
         for yy in range(2):
             for k in range(2):
                 kh[cc, yy, k * half:(k + 1) * half] = kbuf[cc, yy, k, pl.ds(c * half, half)]
-    column = jnp.broadcast_to(v_ref[:, pl.ds(pl.multiple_of(c * half, half), half)], (width, half)).T
-    side[0:half] = column - e_ref[0, 2 * o]
-    side[half:virtuals] = column - e_ref[0, 2 * o + 1]
+    vcol = jnp.broadcast_to(v_ref[:, pl.ds(pl.multiple_of(c * half, half), half)], (width, half)).T
+    side[0:half] = vcol - e_ref[0, 2 * o]
+    side[half:virtuals] = vcol - e_ref[0, 2 * o + 1]
     vrow = v_ref[...]
     rows8 = lax.broadcasted_iota(jnp.int32, cnt_ref.shape, 0)
     lanes8 = lax.broadcasted_iota(jnp.int32, cnt_ref.shape, 1)
@@ -279,38 +308,10 @@
                         w1[k] * part + w2[k] * part.astype(bf16).astype(f32)
                     )
 
-    def place(d, sign):
-        zz = z - d + 2 * d * sign
-        ok = jnp.logical_and(jnp.logical_and(zz >= 0, zz < lines), jnp.logical_or(d > 0, sign == 0))
-        return zz, ok
-
-    def step(d, carry):
-        @pl.when(d < lines)
-        def _():
-            for n in range(2):
-                yy = (y + n) % 2
-                for sign in range(2):
-                    zz, ok = place(d, sign)
-
-                    @pl.when(ok)
-                    def _():
-                        z_copy(0, zz, yy).wait_recv()
-                        forward(zz, yy, sign == 0, sign == 1)
-
-        before = d - 1
-        for sign in range(2):
-            zz, ok = place(before, sign)
-
-            @pl.when(ok)
-            def _():
-                for n in range(2):
-                    yy = (y + n) % 2
-                    x_wait(zz, yy)
-                    s_copy(zz * 2 + ox, yy).start()
-
-        def each(n, carry):
-            zz, ok = place(before, n // 2)
-            oo = zz * 2 + (x + n) % 2
+    def column(d, ox_side):
+        def each(sign, carry):
+            zz, ok = place(d, sign)
+            oo = zz * 2 + (x + ox_side) % 2
 
             @pl.when(ok)
             def _():
@@ -320,10 +321,24 @@
 
             return carry
 
-        lax.fori_loop(0, 4, each, 0)
-        return carry
-
-    lax.fori_loop(1, lines + 1, step, 0)
+        lax.fori_loop(0, 2, each, 0)
+
+    column(0, 0)
+    column(0, 1)
+
+    def step(d, carry):
+        def part(n, carry):
+            @pl.when(d < lines)
+            def _():
+                stage(d, n)
+
+            across(d - 1, n)
+            column(d - 1, n)
+            return carry
+
+        return lax.fori_loop(0, 2, part, carry)
+
+    lax.fori_loop(2, lines + 1, step, 0)
 
     out_width = aux_ref.shape[1]
 

time: 64.5 us -> 62.2 us (0.964)
  Pallas kernels: 60.5 us -> 57.9 us
    pallas_call x1, Pallas kernels: 60.5 us -> 57.9 us  [table_body(): pl.pallas_call(kernel, out_shape=(jax.ShapeDtypeStruct((held, virtuals, w...]
where the time goes in v4:
time: 62.2 us; the launch traced here: 61.7 us
  Pallas kernels  57.9 us (93%)
  local copies, waits for them, and re-layouts  2.56 us (4%)
  between operations  1.3 us (2%)
    pallas_call x1, Pallas kernels, table_body(): pl.pallas_call(kernel, out_shape=(jax.ShapeDtypeStruct((held, virtuals, w...  57.9 us
    unnamed x4, local copies, waits for them, and re-layouts  2.56 us

profile of v4, /device:TPU:3, one launch (start us, length us, event | category | flops | bytes accessed | tf_op | source)
XLA Modules:
  0.0 61.7 jit_solution(3178755897459300133)
XLA Ops:
  1.3 57.9 %shard_map.86 = (f32[2,256,256]{2,1,0:T(8,128)}, f32[256,128]{1,0:T(8,128)}) custom-call(bf16[2,256,256]{2,1,0:T(8,128)(2,1)} %f_hbm.1, f32[1,16]{1,0:T(1,128)} %bitcast.6, f32[1,256]{1,0:T(1,128)} %bitcast.5, s32[1,32]{1,0:T(1,128)} %bitcast.7, s32[1,32]{1,0:T(1,128)} %bitcast.8, s32[1,32]{1,0:T(1,128)} %bitcast.9, s32[1]{0:T(128)S(6)} %copy.11.count_ref), custom_call_target="tpu_custom_call" | custom-call | tf_op jit(solution)/shard_map/pallas_call | solution.py:468
  59.2 0.0 copy-start
  59.2 1.9 %copy.12 = f32[2,256,256]{2,1,0:T(8,128)} copy(f32[2,256,256]{2,1,0:T(8,128)} %get-tuple-element.4) | data formatting | bytes 1048576
  61.1 0.0 copy-done
  61.1 0.7 %copy.13 = f32[256,128]{1,0:T(8,128)} copy(f32[256,128]{1,0:T(8,128)S(1)} %copy-done) | data formatting | bytes 262144
Async XLA Ops:
  59.2 1.9 %copy-start = (f32[256,128]{1,0:T(8,128)S(1)}, f32[256,128]{1,0:T(8,128)}, u32[]{:S(2)}) copy-start(f32[256,128]{1,0:T(8,128)} %get-tuple-element.5) | copy-start | bytes 393220

commit v5 on v4

--- a/solution.py
+++ b/solution.py
@@ -112,9 +112,9 @@
 def kernel(
     f_hbm, e_hbm, v_hbm, i_hbm, j_hbm, partner_hbm, count_ref,
     gamma_ref, aux_ref,
-    kbuf, lbuf, kh, cnt, gacc, gsend, grecv, gfull, gsib, asend, arecv, tsend, trecv,
+    kbuf, lbuf, kh, cnt, gacc, gsend, grecv, gfull, gsib, axsend, axrecv, akeep, azsend, azrecv, tsend, trecv,
     ky_s, ky_r, ksib_s, ksib_r, z_s, z_r, x_s, x_r, s_s, s_r,
-    cnt_s, cnt_r, g_s, g_r, gs_s, gs_r, a_s, a_r, t_s, t_r,
+    cnt_s, cnt_r, g_s, g_r, gs_s, gs_r, ax_s, ax_r, az_s, az_r, t_s, t_r,
     f_ref, e_ref, v_ref, i_ref, j_ref, partner_ref, cnt_ref, side, in_s,
 ):
     occ_count = lax.axis_size("occ")
@@ -351,8 +351,11 @@
     def gs_copy(h):
         return rcopy(gfull.at[h], gsib.at[h], gs_s.at[h], gs_r.at[h], sibling)
 
-    def a_copy(h, oo):
-        return rcopy(asend.at[h, oo], arecv.at[h, o], a_s.at[h, oo], a_r.at[h, o], dev(oo, a))
+    def ax_copy(h, b):
+        return rcopy(axsend.at[h, b], axrecv.at[h, b], ax_s.at[h, b], ax_r.at[h, b], x_peer)
+
+    def az_copy(h, b):
+        return rcopy(azsend.at[h, b], azrecv.at[h, z], az_s.at[h, b], az_r.at[h, z], dev(b * 2 + x, a))
 
     def t_copy(h):
         return rcopy(tsend.at[h], trecv.at[o % 2], t_s.at[h], t_r.at[o % 2], dev(2 * a + h, ta))
@@ -382,25 +385,28 @@
         for n in range(4):
             block = (ta + 2 + n) % 4
             terms = tn(rounded, kbuf[block % 2, block // 2].reshape(held * virtuals, width))
-            for g in range(2):
-                oo = 2 * block + g
-                part = terms[:, cols(g)]
-                asend[h, oo] = part.astype(bf16)
-
-                @pl.when(oo == o)
-                def _():
-                    aux_ref[cols(h)] = part
-
-                @pl.when(oo != o)
-                def _():
-                    a_copy(h, oo).start()
-
-    for h in range(2):
-        total = aux_ref[cols(h)]
-        for s in range(1, occ_count):
-            oo = (o + s) % occ_count
-            rcopy(asend.at[h, oo], arecv.at[h, oo], a_s.at[h, oo], a_r.at[h, oo], dev(oo, a)).wait_recv()
-            total += arecv[h, oo].astype(f32)
+            low, high = terms[:, cols(0)], terms[:, cols(1)]
+            axsend[h, block] = jnp.where(x == 0, high, low).astype(bf16)
+            ax_copy(h, block).start()
+            akeep[h, block] = jnp.where(x == 0, low, high)
+
+    for h in range(2):
+        for n in range(4):
+            block = (ta + 2 + n) % 4
+            ax_copy(h, block).wait_recv()
+            pair = akeep[h, block] + axrecv[h, block].astype(f32)
+            if n == 2:
+                akeep[h, block] = pair
+            else:
+                azsend[h, block] = pair.astype(bf16)
+                az_copy(h, block).start()
+
+    for h in range(2):
+        total = akeep[h, z]
+        for n in range(1, lines):
+            zz = (z + n) % lines
+            rcopy(azsend.at[h, zz], azrecv.at[h, zz], az_s.at[h, zz], az_r.at[h, zz], dev(zz * 2 + x, a)).wait_recv()
+            total += azrecv[h, zz].astype(f32)
         tsend[h] = total
 
         @pl.when(t_far(h))
@@ -431,12 +437,16 @@
     for s in range(1, occ_count):
         oo = (o + s) % occ_count
         cnt_copy(oo).wait_send()
-        a_copy(0, oo).wait_send()
-        a_copy(1, oo).wait_send()
     for h in range(2):
         @pl.when(t_far(h))
         def _():
             t_copy(h).wait_send()
+
+        for n in range(lines):
+            block = (z + n) % lines
+            ax_copy(h, block).wait_send()
+            if n > 0:
+                az_copy(h, block).wait_send()
 
     def drain(zz, carry):
         for yy in range(2):
@@ -483,15 +493,18 @@
             pltpu.VMEM((2, 2, virtuals, out_width), bf16),
             pltpu.VMEM((2, virtuals, out_width), f32),
             pltpu.VMEM((2, virtuals, out_width), f32),
-            pltpu.VMEM((2, occ_count, out_width, out_width), bf16),
-            pltpu.VMEM((2, occ_count, out_width, out_width), bf16),
+            pltpu.VMEM((2, lines, out_width, out_width), bf16),
+            pltpu.VMEM((2, lines, out_width, out_width), bf16),
+            pltpu.VMEM((2, lines, out_width, out_width), f32),
+            pltpu.VMEM((2, lines, out_width, out_width), bf16),
+            pltpu.VMEM((2, lines, out_width, out_width), bf16),
             pltpu.VMEM((2, out_width, out_width), f32),
             pltpu.VMEM((2, out_width, out_width), f32),
             dma((2,)), dma((2,)), dma((4,)), dma((4,)),
             dma((2, lines, 2)), dma((lines, 2)), dma((lines, 2)), dma((lines, 2)),
             dma((occ_count, 2)), dma((occ_count, 2)),
             dma((occ_count,)), dma((occ_count,)), dma((2, 2)), dma((2, 2)), dma((2,)), dma((2,)),
-            dma((2, occ_count)), dma((2, occ_count)), dma((2,)), dma((2,)),
+            dma((2, lines)), dma((2, lines)), dma((2, lines)), dma((2, lines)), dma((2,)), dma((2,)),
             pltpu.VMEM((held, virtuals, width), bf16),
             pltpu.SMEM((1, orbitals), f32),
             pltpu.VMEM((1, virtuals), f32),

time: 62.2 us -> 60.4 us (0.971)
  Pallas kernels: 57.9 us -> 55.8 us
    pallas_call x1, Pallas kernels: 57.9 us -> 55.8 us  [table_body(): pl.pallas_call(kernel, out_shape=(jax.ShapeDtypeStruct((held, virtuals, w...]
where the time goes in v5:
time: 60.4 us; the launch traced here: 59.6 us
  Pallas kernels  55.8 us (92%)
  local copies, waits for them, and re-layouts  2.56 us (4%)
  between operations  1.3 us (2%)
    pallas_call x1, Pallas kernels, table_body(): pl.pallas_call(kernel, out_shape=(jax.ShapeDtypeStruct((held, virtuals, w...  55.8 us
    unnamed x4, local copies, waits for them, and re-layouts  2.56 us

profile of v5, /device:TPU:3, one launch (start us, length us, event | category | flops | bytes accessed | tf_op | source)
XLA Modules:
  0.0 59.6 jit_solution(12044201444767073561)
XLA Ops:
  1.3 55.8 %shard_map.86 = (f32[2,256,256]{2,1,0:T(8,128)}, f32[256,128]{1,0:T(8,128)}) custom-call(bf16[2,256,256]{2,1,0:T(8,128)(2,1)} %f_hbm.1, f32[1,16]{1,0:T(1,128)} %bitcast.6, f32[1,256]{1,0:T(1,128)} %bitcast.5, s32[1,32]{1,0:T(1,128)} %bitcast.7, s32[1,32]{1,0:T(1,128)} %bitcast.8, s32[1,32]{1,0:T(1,128)} %bitcast.9, s32[1]{0:T(128)S(6)} %copy.11.count_ref), custom_call_target="tpu_custom_call" | custom-call | tf_op jit(solution)/shard_map/pallas_call | solution.py:478
  57.0 0.0 copy-start
  57.1 1.9 %copy.12 = f32[2,256,256]{2,1,0:T(8,128)} copy(f32[2,256,256]{2,1,0:T(8,128)} %get-tuple-element.4) | data formatting | bytes 1048576
  59.0 0.0 copy-done
  59.0 0.7 %copy.13 = f32[256,128]{1,0:T(8,128)} copy(f32[256,128]{1,0:T(8,128)S(1)} %copy-done) | data formatting | bytes 262144
Async XLA Ops:
  57.0 1.9 %copy-start = (f32[256,128]{1,0:T(8,128)S(1)}, f32[256,128]{1,0:T(8,128)}, u32[]{:S(2)}) copy-start(f32[256,128]{1,0:T(8,128)} %get-tuple-element.5) | copy-start | bytes 393220

commit v6 on v5

--- a/solution.py
+++ b/solution.py
@@ -112,9 +112,9 @@
 def kernel(
     f_hbm, e_hbm, v_hbm, i_hbm, j_hbm, partner_hbm, count_ref,
     gamma_ref, aux_ref,
-    kbuf, lbuf, kh, cnt, gacc, gsend, grecv, gfull, gsib, axsend, axrecv, akeep, azsend, azrecv, tsend, trecv,
+    kbuf, lbuf, kh, cnt, gacc, gsend, grecv, gfull, gsib, axsend, axrecv, akeep, azsend, azrecv, near, nearin, tsend, trecv,
     ky_s, ky_r, ksib_s, ksib_r, z_s, z_r, x_s, x_r, s_s, s_r,
-    cnt_s, cnt_r, g_s, g_r, gs_s, gs_r, ax_s, ax_r, az_s, az_r, t_s, t_r,
+    cnt_s, cnt_r, g_s, g_r, gs_s, gs_r, ax_s, ax_r, az_s, az_r, t_s, t_r, w_s, w_r, n_s, n_r,
     f_ref, e_ref, v_ref, i_ref, j_ref, partner_ref, cnt_ref, side, in_s,
 ):
     occ_count = lax.axis_size("occ")
@@ -192,6 +192,19 @@
         there = lbuf.at[oo, oc, yy]
         rcopy(there, there, s_s.at[oo, yy], s_r.at[oo, yy], sibling).wait_recv()
 
+    zp = z + 1 - 2 * (z % 2)
+
+    def by_z(zz, yy):
+        return jnp.logical_and(zz == zp, yy == oy)
+
+    def w_copy():
+        there = item(z * 2 + ox, oy)
+        return rcopy(there, there, w_s, w_r, dev(zp * 2 + x, a))
+
+    def w_wait():
+        there = item(zp * 2 + ox, oy)
+        rcopy(there, there, w_s, w_r, dev(zp * 2 + x, a)).wait_recv()
+
     def forward(zz, yy, right, left):
         @pl.when(jnp.logical_and(right, z + 1 < lines))
         def _():
@@ -201,7 +214,10 @@
         def _():
             z_copy(1, zz, yy).start()
 
-        x_copy(zz, yy).start()
+        @pl.when(jnp.logical_not(by_z(zz, yy)))
+        def _():
+            x_copy(zz, yy).start()
+
         s_copy(zz * 2 + x, yy).start()
 
     def place(d, sign):
@@ -224,7 +240,7 @@
         for sign in range(2):
             zz, ok = place(d, sign)
 
-            @pl.when(ok)
+            @pl.when(jnp.logical_and(ok, jnp.logical_not(by_z(zz, yy))))
             def _():
                 x_wait(zz, yy)
                 s_copy(zz * 2 + ox, yy).start()
@@ -313,7 +329,7 @@
             zz, ok = place(d, sign)
             oo = zz * 2 + (x + ox_side) % 2
 
-            @pl.when(ok)
+            @pl.when(jnp.logical_and(ok, jnp.logical_or(ox_side == 0, zz != zp)))
             def _():
                 s_wait(oo, 0)
                 s_wait(oo, 1)
@@ -332,13 +348,26 @@
             def _():
                 stage(d, n)
 
+            @pl.when(jnp.logical_and(d == 2, n == 1))
+            def _():
+                w_copy().start()
+
             across(d - 1, n)
+
+            @pl.when(jnp.logical_and(d == lines, n == 1))
+            def _():
+                w_wait()
+                s_copy(zp * 2 + ox, oy).start()
+
             column(d - 1, n)
             return carry
 
         return lax.fori_loop(0, 2, part, carry)
 
     lax.fori_loop(2, lines + 1, step, 0)
+    s_wait(zp * 2 + ox, 0)
+    s_wait(zp * 2 + ox, 1)
+    work(zp * 2 + ox)
 
     out_width = aux_ref.shape[1]
 
@@ -382,31 +411,37 @@
             gamma_ref[k, pl.ds(oc * half, half), cols(h)] = gsib[h, k * half:(k + 1) * half]
         rounded = gamma_ref[:, :, cols(h)].reshape(held * virtuals, out_width).astype(bf16)
 
-        for n in range(4):
-            block = (ta + 2 + n) % 4
+        for block in ((z + 2) % 4, (z + 3 + 2 * (z % 2)) % 4, zp, z):
             terms = tn(rounded, kbuf[block % 2, block // 2].reshape(held * virtuals, width))
             low, high = terms[:, cols(0)], terms[:, cols(1)]
             axsend[h, block] = jnp.where(x == 0, high, low).astype(bf16)
             ax_copy(h, block).start()
             akeep[h, block] = jnp.where(x == 0, low, high)
 
-    for h in range(2):
-        for n in range(4):
-            block = (ta + 2 + n) % 4
-            ax_copy(h, block).wait_recv()
-            pair = akeep[h, block] + axrecv[h, block].astype(f32)
-            if n == 2:
-                akeep[h, block] = pair
-            else:
-                azsend[h, block] = pair.astype(bf16)
-                az_copy(h, block).start()
+    across_z = (z + 3 + 2 * (z % 2)) % 4
+
+    def near_copy(h):
+        return rcopy(near.at[h], nearin.at[h], n_s.at[h], n_r.at[h], dev(zp * 2 + x, a))
+
+    def pair_sum(h, block):
+        ax_copy(h, block).wait_recv()
+        return akeep[h, block] + axrecv[h, block].astype(f32)
+
+    for h in range(2):
+        for block in ((z + 2) % 4, across_z):
+            azsend[h, block] = pair_sum(h, block).astype(bf16)
+            az_copy(h, block).start()
+        near[h] = pair_sum(h, zp)
+        near_copy(h).start()
+        akeep[h, z] = pair_sum(h, z)
 
     for h in range(2):
         total = akeep[h, z]
-        for n in range(1, lines):
-            zz = (z + n) % lines
+        for zz in ((z + 2) % 4, across_z):
             rcopy(azsend.at[h, zz], azrecv.at[h, zz], az_s.at[h, zz], az_r.at[h, zz], dev(zz * 2 + x, a)).wait_recv()
             total += azrecv[h, zz].astype(f32)
+        near_copy(h).wait_recv()
+        total += nearin[h]
         tsend[h] = total
 
         @pl.when(t_far(h))
@@ -425,6 +460,7 @@
 
         aux_ref[cols(h)] = (tsend[h] + trecv[h].T) * scale
 
+    w_copy().wait_send()
     for r in range(2):
         ky(r).wait_send()
         g_copy(r, 0).wait_send()
@@ -445,8 +481,10 @@
         for n in range(lines):
             block = (z + n) % lines
             ax_copy(h, block).wait_send()
-            if n > 0:
-                az_copy(h, block).wait_send()
+
+        az_copy(h, (z + 2) % 4).wait_send()
+        az_copy(h, across_z).wait_send()
+        near_copy(h).wait_send()
 
     def drain(zz, carry):
         for yy in range(2):
@@ -458,7 +496,10 @@
             def _():
                 z_copy(1, zz, yy).wait_send()
 
-            x_copy(zz, yy).wait_send()
+            @pl.when(jnp.logical_not(by_z(zz, yy)))
+            def _():
+                x_copy(zz, yy).wait_send()
+
             s_copy(zz * 2, yy).wait_send()
             s_copy(zz * 2 + 1, yy).wait_send()
         return carry
@@ -500,11 +541,13 @@
             pltpu.VMEM((2, lines, out_width, out_width), bf16),
             pltpu.VMEM((2, out_width, out_width), f32),
             pltpu.VMEM((2, out_width, out_width), f32),
+            pltpu.VMEM((2, out_width, out_width), f32),
+            pltpu.VMEM((2, out_width, out_width), f32),
             dma((2,)), dma((2,)), dma((4,)), dma((4,)),
             dma((2, lines, 2)), dma((lines, 2)), dma((lines, 2)), dma((lines, 2)),
             dma((occ_count, 2)), dma((occ_count, 2)),
             dma((occ_count,)), dma((occ_count,)), dma((2, 2)), dma((2, 2)), dma((2,)), dma((2,)),
-            dma((2, lines)), dma((2, lines)), dma((2, lines)), dma((2, lines)), dma((2,)), dma((2,)),
+            dma((2, lines)), dma((2, lines)), dma((2, lines)), dma((2, lines)), dma((2,)), dma((2,)), dma, dma, dma((2,)), dma((2,)),
             pltpu.VMEM((held, virtuals, width), bf16),
             pltpu.SMEM((1, orbitals), f32),
             pltpu.VMEM((1, virtuals), f32),

time: 60.4 us -> 61 us (level)
  no operation moved by 1% of the time
where the time goes in v6:
time: 61 us; the launch traced here: 60 us
  Pallas kernels  56.2 us (92%)
  local copies, waits for them, and re-layouts  2.56 us (4%)
  between operations  1.3 us (2%)
    pallas_call x1, Pallas kernels, table_body(): pl.pallas_call(kernel, out_shape=(jax.ShapeDtypeStruct((held, virtuals, w...  56.2 us
    unnamed x4, local copies, waits for them, and re-layouts  2.56 us

profile of v6, /device:TPU:3, one launch (start us, length us, event | category | flops | bytes accessed | tf_op | source)
XLA Modules:
  0.0 60.0 jit_solution(4151266197543101321)
XLA Ops:
  1.3 56.2 %shard_map.86 = (f32[2,256,256]{2,1,0:T(8,128)}, f32[256,128]{1,0:T(8,128)}) custom-call(bf16[2,256,256]{2,1,0:T(8,128)(2,1)} %f_hbm.1, f32[1,16]{1,0:T(1,128)} %bitcast.6, f32[1,256]{1,0:T(1,128)} %bitcast.5, s32[1,32]{1,0:T(1,128)} %bitcast.7, s32[1,32]{1,0:T(1,128)} %bitcast.8, s32[1,32]{1,0:T(1,128)} %bitcast.9, s32[1]{0:T(128)S(6)} %copy.11.count_ref), custom_call_target="tpu_custom_call" | custom-call | tf_op jit(solution)/shard_map/pallas_call | solution.py:519
  57.5 0.0 copy-start
  57.5 1.9 %copy.12 = f32[2,256,256]{2,1,0:T(8,128)} copy(f32[2,256,256]{2,1,0:T(8,128)} %get-tuple-element.4) | data formatting | bytes 1048576
  59.4 0.0 copy-done
  59.4 0.7 %copy.13 = f32[256,128]{1,0:T(8,128)} copy(f32[256,128]{1,0:T(8,128)S(1)} %copy-done) | data formatting | bytes 262144
Async XLA Ops:
  57.5 1.9 %copy-start = (f32[256,128]{1,0:T(8,128)S(1)}, f32[256,128]{1,0:T(8,128)}, u32[]{:S(2)}) copy-start(f32[256,128]{1,0:T(8,128)} %get-tuple-element.5) | copy-start | bytes 393220

commit v7 on v6

--- a/solution.py
+++ b/solution.py
@@ -114,7 +114,7 @@
     gamma_ref, aux_ref,
     kbuf, lbuf, kh, cnt, gacc, gsend, grecv, gfull, gsib, axsend, axrecv, akeep, azsend, azrecv, near, nearin, tsend, trecv,
     ky_s, ky_r, ksib_s, ksib_r, z_s, z_r, x_s, x_r, s_s, s_r,
-    cnt_s, cnt_r, g_s, g_r, gs_s, gs_r, ax_s, ax_r, az_s, az_r, t_s, t_r, w_s, w_r, n_s, n_r,
+    cnt_s, cnt_r, g_s, g_r, gs_s, gs_r, ax_s, ax_r, az_s, az_r, t_s, t_r, n_s, n_r,
     f_ref, e_ref, v_ref, i_ref, j_ref, partner_ref, cnt_ref, side, in_s,
 ):
     occ_count = lax.axis_size("occ")
@@ -194,17 +194,6 @@
 
     zp = z + 1 - 2 * (z % 2)
 
-    def by_z(zz, yy):
-        return jnp.logical_and(zz == zp, yy == oy)
-
-    def w_copy():
-        there = item(z * 2 + ox, oy)
-        return rcopy(there, there, w_s, w_r, dev(zp * 2 + x, a))
-
-    def w_wait():
-        there = item(zp * 2 + ox, oy)
-        rcopy(there, there, w_s, w_r, dev(zp * 2 + x, a)).wait_recv()
-
     def forward(zz, yy, right, left):
         @pl.when(jnp.logical_and(right, z + 1 < lines))
         def _():
@@ -214,10 +203,7 @@
         def _():
             z_copy(1, zz, yy).start()
 
-        @pl.when(jnp.logical_not(by_z(zz, yy)))
-        def _():
-            x_copy(zz, yy).start()
-
+        x_copy(zz, yy).start()
         s_copy(zz * 2 + x, yy).start()
 
     def place(d, sign):
@@ -240,7 +226,7 @@
         for sign in range(2):
             zz, ok = place(d, sign)
 
-            @pl.when(jnp.logical_and(ok, jnp.logical_not(by_z(zz, yy))))
+            @pl.when(ok)
             def _():
                 x_wait(zz, yy)
                 s_copy(zz * 2 + ox, yy).start()
@@ -329,7 +315,7 @@
             zz, ok = place(d, sign)
             oo = zz * 2 + (x + ox_side) % 2
 
-            @pl.when(jnp.logical_and(ok, jnp.logical_or(ox_side == 0, zz != zp)))
+            @pl.when(ok)
             def _():
                 s_wait(oo, 0)
                 s_wait(oo, 1)
@@ -348,26 +334,13 @@
             def _():
                 stage(d, n)
 
-            @pl.when(jnp.logical_and(d == 2, n == 1))
-            def _():
-                w_copy().start()
-
             across(d - 1, n)
-
-            @pl.when(jnp.logical_and(d == lines, n == 1))
-            def _():
-                w_wait()
-                s_copy(zp * 2 + ox, oy).start()
-
             column(d - 1, n)
             return carry
 
         return lax.fori_loop(0, 2, part, carry)
 
     lax.fori_loop(2, lines + 1, step, 0)
-    s_wait(zp * 2 + ox, 0)
-    s_wait(zp * 2 + ox, 1)
-    work(zp * 2 + ox)
 
     out_width = aux_ref.shape[1]
 
@@ -460,7 +433,6 @@
 
         aux_ref[cols(h)] = (tsend[h] + trecv[h].T) * scale
 
-    w_copy().wait_send()
     for r in range(2):
         ky(r).wait_send()
         g_copy(r, 0).wait_send()
@@ -496,10 +468,7 @@
             def _():
                 z_copy(1, zz, yy).wait_send()
 
-            @pl.when(jnp.logical_not(by_z(zz, yy)))
-            def _():
-                x_copy(zz, yy).wait_send()
-
+            x_copy(zz, yy).wait_send()
             s_copy(zz * 2, yy).wait_send()
             s_copy(zz * 2 + 1, yy).wait_send()
         return carry
@@ -547,7 +516,7 @@
             dma((2, lines, 2)), dma((lines, 2)), dma((lines, 2)), dma((lines, 2)),
             dma((occ_count, 2)), dma((occ_count, 2)),
             dma((occ_count,)), dma((occ_count,)), dma((2, 2)), dma((2, 2)), dma((2,)), dma((2,)),
-            dma((2, lines)), dma((2, lines)), dma((2, lines)), dma((2, lines)), dma((2,)), dma((2,)), dma, dma, dma((2,)), dma((2,)),
+            dma((2, lines)), dma((2, lines)), dma((2, lines)), dma((2, lines)), dma((2,)), dma((2,)), dma((2,)), dma((2,)),
             pltpu.VMEM((held, virtuals, width), bf16),
             pltpu.SMEM((1, orbitals), f32),
             pltpu.VMEM((1, virtuals), f32),

time: 61 us -> 60.7 us (level)
  no operation moved by 1% of the time
where the time goes in v7:
time: 60.7 us; the launch traced here: 60.3 us
  Pallas kernels  56.5 us (93%)
  local copies, waits for them, and re-layouts  2.56 us (4%)
  between operations  1.3 us (2%)
    pallas_call x1, Pallas kernels, table_body(): pl.pallas_call(kernel, out_shape=(jax.ShapeDtypeStruct((held, virtuals, w...  56.5 us
    unnamed x4, local copies, waits for them, and re-layouts  2.56 us

profile of v7, /device:TPU:3, one launch (start us, length us, event | category | flops | bytes accessed | tf_op | source)
XLA Modules:
  0.0 60.3 jit_solution(5849793954488515769)
XLA Ops:
  1.3 56.5 %shard_map.86 = (f32[2,256,256]{2,1,0:T(8,128)}, f32[256,128]{1,0:T(8,128)}) custom-call(bf16[2,256,256]{2,1,0:T(8,128)(2,1)} %f_hbm.1, f32[1,16]{1,0:T(1,128)} %bitcast.6, f32[1,256]{1,0:T(1,128)} %bitcast.5, s32[1,32]{1,0:T(1,128)} %bitcast.7, s32[1,32]{1,0:T(1,128)} %bitcast.8, s32[1,32]{1,0:T(1,128)} %bitcast.9, s32[1]{0:T(128)S(6)} %copy.11.count_ref), custom_call_target="tpu_custom_call" | custom-call | tf_op jit(solution)/shard_map/pallas_call | solution.py:488
  57.8 0.0 copy-start
  57.8 1.9 %copy.12 = f32[2,256,256]{2,1,0:T(8,128)} copy(f32[2,256,256]{2,1,0:T(8,128)} %get-tuple-element.4) | data formatting | bytes 1048576
  59.7 0.0 copy-done
  59.7 0.7 %copy.13 = f32[256,128]{1,0:T(8,128)} copy(f32[256,128]{1,0:T(8,128)S(1)} %copy-done) | data formatting | bytes 262144
Async XLA Ops:
  57.8 1.9 %copy-start = (f32[256,128]{1,0:T(8,128)S(1)}, f32[256,128]{1,0:T(8,128)}, u32[]{:S(2)}) copy-start(f32[256,128]{1,0:T(8,128)} %get-tuple-element.5) | copy-start | bytes 393220
